TPU v7x, 32 devices: a whole 2x2x4 slice. The times are simulated.
32 devices in a mesh: dp: 8 (over y, x, core), seq: 4 (over z).
Axes of the slice: x: 2, y: 2, z: 4, core: 2. Of those that a mesh axis runs over, the one named last changes fastest.
Arguments:
- inputs: bfloat16 [32768, 1024], P(('dp', 'seq')), may hold values from -6 to 6
- timestep: bfloat16 [8, 1024], P('dp'), may hold values from -6 to 6
- context_len: int32 [8, 8], P('dp'), may hold values from 0 to 475, as said below
- out_grad: bfloat16 [32768, 1024], P(('dp', 'seq')), may hold values from -6 to 6
- qkv_weight: bfloat16 [1024, 3072], P(('dp', 'seq')), may hold values from -0.1875 to 0.1875
- out_weight: bfloat16 [1024, 1024], P(('dp', 'seq')), may hold values from -0.75 to 0.75
- in_weight: bfloat16 [1024, 4096], P(('dp', 'seq')), may hold values from -0.1875 to 0.1875
- back_weight: bfloat16 [4096, 1024], P(('dp', 'seq')), may hold values from -0.09375 to 0.09375
- vectors: bfloat16 [1024, 8], P(('dp', 'seq')), may hold values from -1.25 to 1.4
- bias_ff: bfloat16 [4096], P(('dp', 'seq')), may hold values from -3 to 3
Outputs:
- result: float32 [32768, 1024], P(('dp', 'seq'))
- grad_input: float32 [32768, 1024], P(('dp', 'seq'))
- grad_qkv: float32 [1024, 3072], P(('dp', 'seq'))
- grad_out: float32 [1024, 1024], P(('dp', 'seq'))
- grad_in: float32 [1024, 4096], P(('dp', 'seq'))
- grad_back: float32 [4096, 1024], P(('dp', 'seq'))
- grad_vectors: float32 [1024, 8], P(('dp', 'seq'))
- grad_bias_ff: float32 [4096], P(('dp', 'seq'))
Inputs may be any that keep to these rules, and one draw needn't show every extreme that they name: `context_len`: some slot has exactly 475 context tokens.
All inputs are finite; a program needn't handle non-finite values.
Results may differ from a plain program's by a relative error of at most 0.012.
The roundings to bfloat16 on the way count: a program that leaves them out, or rounds other values in their place, can miss the bound.
Values may be sent and summed in bfloat16 or wider, within the bound.
A program may use at most 256 MiB of HBM per device.

v0:
```python
import math

import jax
import jax.numpy as jnp
from jax import lax
from jax.sharding import PartitionSpec as P

HEAD_DIM = 64
SLOT = 512
BLOCK = 25


norm_eps = 1e-05


def norm_forward(resid, gain_vec, shift_vec):
    row_mean = jnp.mean(resid, axis=-1, keepdims=True)
    centered = resid - row_mean
    variance = jnp.mean(centered * centered, axis=-1, keepdims=True)
    inv_std = lax.rsqrt(variance + norm_eps)
    normed = centered * inv_std
    return (normed * gain_vec + shift_vec, normed, inv_std)


def norm_backward(grad_out, normed, inv_std, gain_vec):
    grad_norm = grad_out * gain_vec
    grad_resid = inv_std * (
        grad_norm
        - jnp.mean(grad_norm, axis=-1, keepdims=True)
        - normed * jnp.mean(grad_norm * normed, axis=-1, keepdims=True)
    )
    return (grad_resid, jnp.sum(grad_out * normed, axis=0), jnp.sum(grad_out, axis=0))


def gelu_slope(pre_act):
    return 0.5 * (1.0 + lax.erf(pre_act * math.sqrt(0.5))) + pre_act * jnp.exp(
        -0.5 * pre_act * pre_act
    ) / math.sqrt(2.0 * math.pi)


def slot_scores(queries, key_vecs, live_len):
    inv_root = 1.0 / math.sqrt(HEAD_DIM)
    raw_scores = (
        jnp.einsum("qhd,khd->hqk", queries, key_vecs, preferred_element_type=jnp.float32) * inv_root
    )
    key_valid = jnp.arange(SLOT, dtype=jnp.int32) < live_len
    return jnp.where(key_valid[None, None, :], raw_scores, -1e30)


def slot_forward(parts):
    queries, key_vecs, values, live_len = parts
    masked = slot_scores(queries, key_vecs, live_len)
    row_max = jnp.max(masked, axis=-1, keepdims=True)
    exp_scores = jnp.exp(masked - row_max)
    exp_total = jnp.sum(exp_scores, axis=-1, keepdims=True)
    attn_probs = (exp_scores / exp_total).astype(jnp.bfloat16)
    context = jnp.einsum("hqk,khd->qhd", attn_probs, values, preferred_element_type=jnp.float32)
    return (context.astype(jnp.bfloat16), (row_max + jnp.log(exp_total))[..., 0])


def slot_backward(parts):
    queries, key_vecs, values, live_len, log_total, grad_ctx = parts
    inv_root = 1.0 / math.sqrt(HEAD_DIM)
    masked = slot_scores(queries, key_vecs, live_len)
    attn_exact = jnp.exp(masked - log_total[..., None])
    attn_probs = attn_exact.astype(jnp.bfloat16)
    grad_probs = jnp.einsum("qhd,khd->hqk", grad_ctx, values, preferred_element_type=jnp.float32)
    row_dot = jnp.sum(attn_exact * grad_probs, axis=-1, keepdims=True)
    grad_scores = (attn_exact * (grad_probs - row_dot)).astype(jnp.bfloat16)
    grad_query = (
        jnp.einsum("hqk,khd->qhd", grad_scores, key_vecs, preferred_element_type=jnp.float32)
        * inv_root
    )
    grad_key = (
        jnp.einsum("hqk,qhd->khd", grad_scores, queries, preferred_element_type=jnp.float32)
        * inv_root
    )
    grad_value = jnp.einsum(
        "hqk,qhd->khd", attn_probs, grad_ctx, preferred_element_type=jnp.float32
    )
    return (
        grad_query.astype(jnp.bfloat16),
        grad_key.astype(jnp.bfloat16),
        grad_value.astype(jnp.bfloat16),
    )


def shards(
    inputs,
    timestep,
    context_len,
    out_grad,
    qkv_weight,
    out_weight,
    in_weight,
    back_weight,
    vectors,
    bias_ff,
):
    qkv_full, out_full, in_full, back_full, vec_full, bias_full = (
        lax.all_gather(qkv_weight, ("dp", "seq"), axis=0, tiled=True),
        lax.all_gather(out_weight, ("dp", "seq"), axis=0, tiled=True),
        lax.all_gather(in_weight, ("dp", "seq"), axis=0, tiled=True),
        lax.all_gather(back_weight, ("dp", "seq"), axis=0, tiled=True),
        lax.all_gather(vectors, ("dp", "seq"), axis=0, tiled=True),
        lax.all_gather(bias_ff, ("dp", "seq"), axis=0, tiled=True),
    )
    vec_all = vec_full.astype(jnp.float32)
    bias_all = bias_full.astype(jnp.float32)
    width = inputs.shape[1]
    resid_in = inputs.astype(jnp.float32) + timestep.astype(jnp.float32)
    layer_in = resid_in.astype(jnp.bfloat16)
    qkv_proj = jnp.dot(layer_in, qkv_full, preferred_element_type=jnp.float32)
    queries = (qkv_proj[:, :width] + vec_all[:, 0]).astype(jnp.bfloat16)
    key_vecs = qkv_proj[:, width : 2 * width].astype(jnp.bfloat16)
    values = (qkv_proj[:, 2 * width :] + vec_all[:, 1]).astype(jnp.bfloat16)
    q_heads, k_heads, v_heads = (
        lax.all_to_all(queries, "seq", split_axis=1, concat_axis=0, tiled=True),
        lax.all_to_all(key_vecs, "seq", split_axis=1, concat_axis=0, tiled=True),
        lax.all_to_all(values, "seq", split_axis=1, concat_axis=0, tiled=True),
    )
    slot_count = context_len.shape[1]
    head_width = q_heads.shape[1]
    slot_shape = (slot_count, SLOT, head_width // HEAD_DIM, HEAD_DIM)
    live_lens = context_len[0] + BLOCK
    q_slots = q_heads.reshape(slot_shape)
    k_slots = k_heads.reshape(slot_shape)
    v_slots = v_heads.reshape(slot_shape)
    ctx_slots, log_totals = lax.map(slot_forward, (q_slots, k_slots, v_slots, live_lens))
    ctx_tokens = lax.all_to_all(
        ctx_slots.reshape(slot_count * SLOT, head_width),
        "seq",
        split_axis=0,
        concat_axis=1,
        tiled=True,
    )
    attn_out = jnp.dot(ctx_tokens, out_full, preferred_element_type=jnp.float32) + vec_all[:, 2]
    normed_mid, unit_mid, inv_mid = norm_forward(resid_in + attn_out, vec_all[:, 4], vec_all[:, 5])
    mid_low = normed_mid.astype(jnp.bfloat16)
    pre_act = jnp.dot(mid_low, in_full, preferred_element_type=jnp.float32) + bias_all
    hidden = jax.nn.gelu(pre_act, approximate=False).astype(jnp.bfloat16)
    branch = jnp.dot(hidden, back_full, preferred_element_type=jnp.float32) + vec_all[:, 3]
    result, unit_out, inv_out = norm_forward(normed_mid + branch, vec_all[:, 6], vec_all[:, 7])
    grad_two, gain_out_grad, shift_out_grad = norm_backward(
        out_grad.astype(jnp.float32), unit_out, inv_out, vec_all[:, 6]
    )
    branch_low = grad_two.astype(jnp.bfloat16)
    grad_backw = jnp.einsum("tf,td->fd", hidden, branch_low, preferred_element_type=jnp.float32)
    grad_hidden = jnp.einsum("td,fd->tf", branch_low, back_full, preferred_element_type=jnp.float32)
    grad_pre = grad_hidden * gelu_slope(pre_act)
    bias_grad = jnp.sum(grad_pre, axis=0)
    pre_low = grad_pre.astype(jnp.bfloat16)
    grad_inw = jnp.einsum("td,tf->df", mid_low, pre_low, preferred_element_type=jnp.float32)
    grad_mid = grad_two + jnp.einsum(
        "tf,df->td", pre_low, in_full, preferred_element_type=jnp.float32
    )
    grad_one, gain_mid_grad, shift_mid_grad = norm_backward(
        grad_mid, unit_mid, inv_mid, vec_all[:, 4]
    )
    attn_low = grad_one.astype(jnp.bfloat16)
    grad_outw = jnp.einsum("td,te->de", ctx_tokens, attn_low, preferred_element_type=jnp.float32)
    grad_ctx = jnp.einsum(
        "te,de->td", attn_low, out_full, preferred_element_type=jnp.float32
    ).astype(jnp.bfloat16)
    grad_ctx_heads = lax.all_to_all(grad_ctx, "seq", split_axis=1, concat_axis=0, tiled=True)
    grad_q, grad_k, grad_v = lax.map(
        slot_backward,
        (q_slots, k_slots, v_slots, live_lens, log_totals, grad_ctx_heads.reshape(slot_shape)),
    )
    token_shape = (slot_count * SLOT, head_width)
    grad_q_tok, grad_k_tok, grad_v_tok = (
        lax.all_to_all(grad_q.reshape(token_shape), "seq", split_axis=0, concat_axis=1, tiled=True),
        lax.all_to_all(grad_k.reshape(token_shape), "seq", split_axis=0, concat_axis=1, tiled=True),
        lax.all_to_all(grad_v.reshape(token_shape), "seq", split_axis=0, concat_axis=1, tiled=True),
    )
    grad_proj = jnp.concatenate([grad_q_tok, grad_k_tok, grad_v_tok], axis=1)
    grad_qkvw = jnp.einsum("td,te->de", layer_in, grad_proj, preferred_element_type=jnp.float32)
    grad_input = grad_one + jnp.einsum(
        "te,de->td", grad_proj, qkv_full, preferred_element_type=jnp.float32
    )
    vec_grads = jnp.stack(
        [
            jnp.sum(grad_q_tok.astype(jnp.float32), axis=0),
            jnp.sum(grad_v_tok.astype(jnp.float32), axis=0),
            jnp.sum(grad_one, axis=0),
            jnp.sum(grad_two, axis=0),
            gain_mid_grad,
            shift_mid_grad,
            gain_out_grad,
            shift_out_grad,
        ],
        axis=1,
    )
    share_qkv, share_out, share_in, share_back, share_vec, share_bias = (
        lax.psum_scatter(grad_qkvw, ("dp", "seq"), scatter_dimension=0, tiled=True),
        lax.psum_scatter(grad_outw, ("dp", "seq"), scatter_dimension=0, tiled=True),
        lax.psum_scatter(grad_inw, ("dp", "seq"), scatter_dimension=0, tiled=True),
        lax.psum_scatter(grad_backw, ("dp", "seq"), scatter_dimension=0, tiled=True),
        lax.psum_scatter(vec_grads, ("dp", "seq"), scatter_dimension=0, tiled=True),
        lax.psum_scatter(bias_grad, ("dp", "seq"), scatter_dimension=0, tiled=True),
    )
    return (result, grad_input, share_qkv, share_out, share_in, share_back, share_vec, share_bias)


def solution(mesh):
    return jax.shard_map(
        shards,
        mesh=mesh,
        in_specs=(
            P(("dp", "seq"), None),
            P("dp", None),
            P("dp", None),
            P(("dp", "seq"), None),
            P(("dp", "seq"), None),
            P(("dp", "seq"), None),
            P(("dp", "seq"), None),
            P(("dp", "seq"), None),
            P(("dp", "seq"), None),
            P(("dp", "seq")),
        ),
        out_specs=(
            P(("dp", "seq"), None),
            P(("dp", "seq"), None),
            P(("dp", "seq"), None),
            P(("dp", "seq"), None),
            P(("dp", "seq"), None),
            P(("dp", "seq"), None),
            P(("dp", "seq"), None),
            P(("dp", "seq")),
        ),
        check_vma=False,
    )
```

profile of v0, /device:TPU:0, one launch (start us, length us, event | category | flops | bytes accessed | tf_op | source)
XLA Modules:
  0.0 2084.1 jit_solution(11017736958252563016)
XLA Ops:
  9.4 71.2 %all-gather = bf16[32,32,8]{1,2,0:T(8,128)(2,1)S(1)} all-gather(bf16[1,32,8]{1,2,0:T(8,128)(2,1)} %bitcast.241), channel_id=1, replica_groups=mesh['dp'=8,'seq'=4] {'dp','seq'}, dimensions={0}, use_global_device_ids=true | all-gather | bytes 16896 | tf_op jit(solution)/shard_map/all_gather | solution.py:105
  84.4 9.1 fusion.102
  108.8 50.6 %all-to-all-done = bf16[1024,4,256]{0,2,1:T(8,128)(2,1)S(1)} async-done(((bf16[1024,4,256]{0,2,1:T(8,128)(2,1)}), bf16[1024,4,256]{0,2,1:T(8,128)(2,1)S(1)}, u32[]{:S(2)}, u32[]{:S(2)}) %all-to-all-start) | async-done | bytes 2097184 | tf_op jit(solution)/shard_map/all_to_all | solution.py:120
  171.6 45.2 %all-to-all-done.1 = bf16[1024,4,256]{0,2,1:T(8,128)(2,1)} async-done(((bf16[1024,4,256]{0,2,1:T(8,128)(2,1)}), bf16[1024,4,256]{0,2,1:T(8,128)(2,1)}, u32[]{:S(2)}, u32[]{:S(2)}) %all-to-all-start.1) | async-done | bytes 2097184 | tf_op jit(solution)/shard_map/all_to_all | solution.py:118
  237.2 59.5 %all-to-all-done.2 = bf16[1024,4,256]{0,2,1:T(8,128)(2,1)} async-done(((bf16[1024,4,256]{0,2,1:T(8,128)(2,1)}), bf16[1024,4,256]{0,2,1:T(8,128)(2,1)}, u32[]{:S(2)}, u32[]{:S(2)}) %all-to-all-start.2) | async-done | bytes 2097184 | tf_op jit(solution)/shard_map/all_to_all | solution.py:119
  310.4 61.0 %while.26 = (s32[]{:T(128)}, bf16[8,512,4,64]{1,3,2,0:T(8,128)(2,1)}, f32[8,4,512]{2,1,0:T(4,128)}, bf16[8,512,4,64]{1,3,2,0:T(8,128)(2,1)}, s32[8]{0:T(128)S(1)...) while((s32[]{:T(128)}, bf16[8,512,4,64]{1,3,2,0:T(8,128)(2,1)}, ...), condition=%wide.region_3.4_spmd, body=%wide.region_0.3_spmd.sunk | while | flops 281147904 | bytes 13701733 | solution.py:129
  371.4 4.8 copy.111
  388.8 104.9 %all-gather.1 = bf16[32,1,128]{2,1,0:T(2,128)(2,1)S(1)} all-gather(bf16[1,1,128]{2,1,0:T(2,128)(2,1)S(1)} %bitcast.242), channel_id=1, replica_groups=mesh['dp'=8,'seq'=4] {'dp','seq'}, dimensions={0}, use_global_device_ids=true | all-gather | bytes 8448 | tf_op jit(solution)/shard_map/all_gather | solution.py:106
  496.6 5.6 fusion.114
  504.9 47.2 %fusion.61 = (bf16[1024,4096]{1,0:T(8,128)(2,1)}, f32[1024,4096]{1,0:T(8,128)}) fusion(f32[4096]{0:T(1024)S(1)} %bitcast.232, bf16[1024,4096]{1,0:T(8,128)(2,1)} %all-gather.11.cloned.1.call-done, bf16[1024,1024]{0,1:T(8,128)(2,1)S(1)} %fusion.108.clone.4), kind=kOutput, calls=%fused_computation.68 | convolution fusion | flops 8866758656 | bytes 35667968 | tf_op jit(solution)/shard_map/dot_general | solution.py:140
  552.1 15.3 fusion.115
  571.6 22.7 %fusion.116 = (f32[4096]{0:T(1024)}, bf16[1024,4096]{1,0:T(8,128)(2,1)}) fusion(f32[1024,4096]{1,0:T(8,128)} %get-tuple-element.251, f32[4096]{0:T(1024)S(1)} %bitcast.233, bf16[4096,1024]{1,0:T(8,128)(2,1)} %all-gather.13.cloned.1.call-done, f32[1024]{0:T(1024)S(1)} %get-tuple-element.257, f32[1024,1024]{0,1:T(8,128)S(1)} %get-tuple-element.253, ...), kind=kOutput, calls=%fused_computation.155 | convolution fusion | flops 8649699328 | bytes 39899136 | tf_op jit(solution)/shard_map/td,fd->tf/dot_general | solution.py:149
  594.3 16.6 multiply_reduce_fusion.1
  614.9 46.6 %all_to_all.140 = bf16[1024,4,256]{0,2,1:T(8,128)(2,1)S(1)} all-to-all(bf16[1024,4,256]{0,2,1:T(8,128)(2,1)S(1)} %bitcast.207), channel_id=1, replica_groups=mesh['dp'=8,'seq'=4] {'seq'}, dimensions={1} | all-to-all | bytes 4194304 | tf_op jit(solution)/shard_map/all_to_all | solution.py:165
  672.2 114.0 %while.27 = (s32[]{:T(128)}, bf16[8,512,4,64]{1,3,2,0:T(8,128)(2,1)S(1)}, bf16[8,512,4,64]{1,3,2,0:T(8,128)(2,1)}, bf16[8,512,4,64]{1,3,2,0:T(8,128)(2,1)}, bf16...) while((s32[]{:T(128)}, ...), condition=%wide.region_14.15_spmd, body=%wide.region_12.14_spmd.sunk | while | flops 687471104 | bytes 34143360 | solution.py:166
  793.8 4.9 all-to-all-start.5
  807.7 36.9 %all-to-all-done.5 = bf16[4,1024,256]{1,2,0:T(8,128)(2,1)} async-done(((bf16[4,1024,256]{1,2,0:T(8,128)(2,1)}), bf16[4,1024,256]{1,2,0:T(8,128)(2,1)}, u32[]{:S(2)}, u32[]{:S(2)}) %all-to-all-start.5) | async-done | bytes 2097184 | tf_op jit(solution)/shard_map/all_to_all | solution.py:172
  849.1 5.6 fusion.80
  856.6 40.1 %all-to-all-done.7 = bf16[4,1024,256]{1,2,0:T(8,128)(2,1)} async-done(((bf16[4,1024,256]{1,2,0:T(8,128)(2,1)}), bf16[4,1024,256]{1,2,0:T(8,128)(2,1)}, u32[]{:S(2)}, u32[]{:S(2)}) %all-to-all-start.7) | async-done | bytes 2097184 | tf_op jit(solution)/shard_map/all_to_all | solution.py:174
  899.9 7.2 fusion.95
  917.9 54.6 %all_to_all.141 = bf16[4,1024,256]{1,2,0:T(8,128)(2,1)S(1)} all-to-all(bf16[4,1024,256]{1,2,0:T(8,128)(2,1)S(1)} %copy.124), channel_id=1, replica_groups=mesh['dp'=8,'seq'=4] {'seq'}, dimensions={0} | all-to-all | bytes 4194304 | tf_op jit(solution)/shard_map/all_to_all | solution.py:173
  973.9 11.9 fusion.89
  985.9 17.3 fusion.98
  1003.9 16.8 fusion.83
  1020.8 5.5 copy.132
  1026.3 42.0 %all-reduce = f32[4096]{0:T(1024)S(1)} all-reduce(f32[4096]{0:T(1024)S(1)} %copy-done.17), channel_id=7, replica_groups=mesh['dp'=8,'seq'=4] {'dp','seq'}, use_global_device_ids=true, to_apply=%region_29.30.clone | all-reduce | flops 4096 | bytes 32768
  1068.9 12.4 fusion.94
  1081.3 5.4 copy.133
  1088.0 96.1 %reduce-scatter.10.cloned.1.call-done = f32[32,1024]{1,0:T(8,128)} async-done(((f32[1024,1024]{1,0:T(8,128)}), f32[32,1024]{1,0:T(8,128)}) %reduce-scatter.10.cloned.1.call-update) | async-done | bytes 131088 | tf_op jit(solution)/shard_map/reduce_scatter | solution.py:196
  1184.1 162.0 %reduce-scatter.8.cloned.1.call-done = f32[32,3072]{1,0:T(8,128)} async-done(((f32[1024,3072]{1,0:T(8,128)}), f32[32,3072]{1,0:T(8,128)}) %reduce-scatter.8.cloned.1.call-update) | async-done | bytes 393232 | tf_op jit(solution)/shard_map/reduce_scatter | solution.py:195
  1346.0 366.2 %reduce-scatter.14.cloned.1.call-done = f32[128,1024]{1,0:T(8,128)} async-done(((f32[4096,1024]{1,0:T(8,128)}), f32[128,1024]{1,0:T(8,128)}) %reduce-scatter.14.cloned.1.call-update) | async-done | bytes 524304 | tf_op jit(solution)/shard_map/reduce_scatter | solution.py:198
  1712.2 365.1 %reduce-scatter.12.cloned.1.call-done = f32[32,4096]{1,0:T(8,128)} async-done(((f32[1024,4096]{1,0:T(8,128)}), f32[32,4096]{1,0:T(8,128)}) %reduce-scatter.12.cloned.1.call-update) | async-done | bytes 524304 | tf_op jit(solution)/shard_map/reduce_scatter | solution.py:197
  (265 shorter events, 320.0 us)
Async XLA Ops:
  7.2 76.5 %copy-start.19 = (bf16[1,1024]{1,0:T(2,128)(2,1)S(1)}, bf16[1,1024]{1,0:T(2,128)(2,1)}, u32[]{:S(2)}) copy-start(bf16[1,1024]{1,0:T(2,128)(2,1)} %param.15) | copy-start | bytes 6148
  7.2 77.2 %all-gather.7.cloned.1.call-start = ((), (), s32[]{:S(2)}) async-start(), calls=%async_computation.13 | async-start | bytes 6488064 | tf_op jit(solution)/shard_map/all_gather | solution.py:101
  7.9 488.6 %all-gather.9.cloned.1.call-start = ((), (), s32[]{:S(2)}) async-start(), calls=%async_computation.14 | async-start | bytes 2162688 | tf_op jit(solution)/shard_map/all_gather | solution.py:102
  8.7 496.2 %all-gather.11.cloned.1.call-start = ((), (), s32[]{:S(2)}) async-start(), calls=%async_computation.15 | async-start | bytes 8650752 | tf_op jit(solution)/shard_map/all_gather | solution.py:103
  83.7 9.8 copy-start.9
  83.7 412.9 %copy-start.20 = (f32[1,1024]{1,0:T(1,128)}, f32[1,1024]{1,0:T(1,128)S(1)}, u32[]{:S(2)}) copy-start(f32[1,1024]{1,0:T(1,128)S(1)} %add.188) | copy-start | bytes 12292
  84.4 467.7 %copy-start.14 = (f32[1024,1]{0,1:T(1,128)}, f32[1024,1]{0,1:T(1,128)S(1)}, u32[]{:S(2)}) copy-start(f32[1024,1]{0,1:T(1,128)S(1)} %get-tuple-element.243) | copy-start | bytes 12292
  101.2 58.2 %all-to-all-start = ((bf16[1024,4,256]{0,2,1:T(8,128)(2,1)}), bf16[1024,4,256]{0,2,1:T(8,128)(2,1)S(1)}, u32[]{:S(2)}, u32[]{:S(2)}) async-start(bf16[1024,4,256]{0,2,1:T(8,128)(2,1)} %bitcast.203), calls=%async_computation | async-start | bytes 4194304 | tf_op jit(solution)/shard_map/all_to_all | solution.py:120
  159.3 57.5 %all-to-all-start.1 = ((bf16[1024,4,256]{0,2,1:T(8,128)(2,1)}), bf16[1024,4,256]{0,2,1:T(8,128)(2,1)}, u32[]{:S(2)}, u32[]{:S(2)}) async-start(bf16[1024,4,256]{0,2,1:T(8,128)(2,1)} %bitcast.202), calls=%async_computation.1 | async-start | bytes 4194304 | tf_op jit(solution)/shard_map/all_to_all | solution.py:118
  167.7 54.4 %copy-start.24 = (s32[1,8]{1,0:T(1,128)S(1)}, s32[1,8]{1,0:T(1,128)}, u32[]{:S(2)}) copy-start(s32[1,8]{1,0:T(1,128)} %param.16) | copy-start | bytes 100
  216.9 79.9 %all-to-all-start.2 = ((bf16[1024,4,256]{0,2,1:T(8,128)(2,1)}), bf16[1024,4,256]{0,2,1:T(8,128)(2,1)}, u32[]{:S(2)}, u32[]{:S(2)}) async-start(bf16[1024,4,256]{0,2,1:T(8,128)(2,1)} %bitcast.201), calls=%async_computation.2 | async-start | bytes 4194304 | tf_op jit(solution)/shard_map/all_to_all | solution.py:119
  221.4 330.7 %all-gather.13.cloned.1.call-start = ((), (), s32[]{:S(2)}) async-start(), calls=%async_computation.16 | async-start | bytes 8650752 | tf_op jit(solution)/shard_map/all_gather | solution.py:104
  371.4 9.2 copy-start.5
  371.4 9.2 copy-start.25
  380.7 8.2 copy-start.22
  384.2 109.5 %copy-start.8 = (bf16[1024,1024]{1,0:T(8,128)(2,1)S(1)}, bf16[1024,1024]{1,0:T(8,128)(2,1)}, u32[]{:S(2)}) copy-start(bf16[1024,1024]{1,0:T(8,128)(2,1)} %param.17) | copy-start | bytes 6291460
  384.2 112.3 %all-to-all-start.3 = ((bf16[4,1024,256]{1,2,0:T(8,128)(2,1)}), bf16[4,1024,256]{1,2,0:T(8,128)(2,1)}, u32[]{:S(2)}, u32[]{:S(2)}) async-start(bf16[4,1024,256]{1,2,0:T(8,128)(2,1)} %copy.112), calls=%async_computation.3 | async-start | bytes 4194304 | tf_op jit(solution)/shard_map/all_to_all | solution.py:130
  504.9 47.2 %copy-start.18 = (f32[1024,1]{0,1:T(1,128)S(1)}, f32[1024,1]{0,1:T(1,128)}, u32[]{:S(2)}) copy-start(f32[1024,1]{0,1:T(1,128)} %get-tuple-element.242) | copy-start | bytes 12292
  567.5 26.8 %copy-start = (f32[1024,1024]{0,1:T(8,128)}, f32[1024,1024]{0,1:T(8,128)S(1)}, u32[]{:S(2)}) copy-start(f32[1024,1024]{0,1:T(8,128)S(1)} %get-tuple-element.253) | copy-start | bytes 12582916
  571.6 22.7 %copy-start.2 = (f32[1024,1024]{0,1:T(8,128)S(1)}, f32[1024,1024]{0,1:T(8,128)}, u32[]{:S(2)}) copy-start(f32[1024,1024]{0,1:T(8,128)} %copy-done.1) | copy-start | bytes 12582916
  793.8 50.8 %all-to-all-start.5 = ((bf16[4,1024,256]{1,2,0:T(8,128)(2,1)}), bf16[4,1024,256]{1,2,0:T(8,128)(2,1)}, u32[]{:S(2)}, u32[]{:S(2)}) async-start(bf16[4,1024,256]{1,2,0:T(8,128)(2,1)} %copy.122), calls=%async_computation.5 | async-start | bytes 4194304 | tf_op jit(solution)/shard_map/all_to_all | solution.py:172
  804.0 45.1 %copy-start.4 = (bf16[1024,1024]{0,1:T(8,128)(2,1)S(1)}, bf16[1024,1024]{0,1:T(8,128)(2,1)}, u32[]{:S(2)}) copy-start(bf16[1024,1024]{0,1:T(8,128)(2,1)} %copy.114) | copy-start | bytes 6291460
  804.0 45.1 %copy-start.16 = (f32[1024,1]{0,1:T(1,128)S(1)}, f32[1024,1]{0,1:T(1,128)}, u32[]{:S(2)}) copy-start(f32[1024,1]{0,1:T(1,128)} %get-tuple-element.241) | copy-start | bytes 12292
  844.5 52.2 %all-to-all-start.7 = ((bf16[4,1024,256]{1,2,0:T(8,128)(2,1)}), bf16[4,1024,256]{1,2,0:T(8,128)(2,1)}, u32[]{:S(2)}, u32[]{:S(2)}) async-start(bf16[4,1024,256]{1,2,0:T(8,128)(2,1)} %copy.126), calls=%async_computation.7 | async-start | bytes 4194304 | tf_op jit(solution)/shard_map/all_to_all | solution.py:174
  849.0 237.6 %reduce-scatter.16.cloned.1.call-start = ((), (), s32[]{:S(2)}) async-start(), calls=%async_computation.21 | async-start | bytes 540672
  899.9 284.2 %reduce-scatter.10.cloned.1.call-start = ((), (), s32[]{:S(2)}) async-start(), calls=%async_computation.18 | async-start | bytes 4325376 | tf_op jit(solution)/shard_map/reduce_scatter | solution.py:196
  907.1 439.0 %reduce-scatter.8.cloned.1.call-start = ((), (), s32[]{:S(2)}) async-start(), calls=%async_computation.17 | async-start | bytes 12976128 | tf_op jit(solution)/shard_map/reduce_scatter | solution.py:195
  915.6 58.3 %copy-start.10 = (bf16[1024,1024]{0,1:T(8,128)(2,1)S(1)}, bf16[1024,1024]{0,1:T(8,128)(2,1)}, u32[]{:S(2)}) copy-start(bf16[1024,1024]{0,1:T(8,128)(2,1)} %copy-done.9) | copy-start | bytes 6291460
  915.6 58.3 %copy-start.21 = (f32[1,1024]{1,0:T(1,128)S(1)}, f32[1,1024]{1,0:T(1,128)}, u32[]{:S(2)}) copy-start(f32[1,1024]{1,0:T(1,128)} %copy-done.20) | copy-start | bytes 12292
  985.8 726.4 %reduce-scatter.14.cloned.1.call-start = ((), (), s32[]{:S(2)}) async-start(), calls=%async_computation.20 | async-start | bytes 17301504 | tf_op jit(solution)/shard_map/reduce_scatter | solution.py:198
  1003.2 1074.1 %reduce-scatter.12.cloned.1.call-start = ((), (), s32[]{:S(2)}) async-start(), calls=%async_computation.19 | async-start | bytes 17301504 | tf_op jit(solution)/shard_map/reduce_scatter | solution.py:197
  1020.8 48.1 %copy-start.12 = (bf16[4,1024,256]{1,2,0:T(8,128)(2,1)S(1)}, bf16[4,1024,256]{1,2,0:T(8,128)(2,1)}, u32[]{:S(2)}) copy-start(bf16[4,1024,256]{1,2,0:T(8,128)(2,1)} %copy-done.11) | copy-start | bytes 6291460
  (10 other events, 28.4 us)
Sparse Core Ops, SparseCore 0:
  10.9 72.2 all-gather.6
  86.2 78.5 all-gather.8
  167.7 128.8 all-gather.10
  299.4 77.3 all-gather.12
  900.0 136.9 reduce-scatter.15
  1039.8 144.2 reduce-scatter.9
  1191.7 154.2 reduce-scatter.7
  1348.9 363.2 reduce-scatter.13
  1715.1 362.1 reduce-scatter.11
where the time goes:
time: 2090 us; the launch traced here: 2080 us
  waiting for transfers between devices  1220 us (58%)
  blocking collectives  319 us (15%)
  matrix products  311 us (15%)
  local copies, waits for them, and re-layouts  138 us (7%)
  other arithmetic  50.4 us (2%)
  starting transfers between devices  26.9 us (1%)
    reduce_scatter x1, waiting for transfers between devices, shards(): lax.psum_scatter(grad_backw, ('dp', 'seq'), scatter_dimension=0, tiled=True)  366 us
    reduce_scatter x1, waiting for transfers between devices, shards(): lax.psum_scatter(grad_inw, ('dp', 'seq'), scatter_dimension=0, tiled=True)  365 us
    reduce_scatter x1, waiting for transfers between devices, shards(): lax.psum_scatter(grad_qkvw, ('dp', 'seq'), scatter_dimension=0, tiled=True)  162 us
    all_gather x1, blocking collectives, shards(): lax.all_gather(bias_ff, ('dp', 'seq'), axis=0, tiled=True)  105 us
    reduce_scatter x1, waiting for transfers between devices, shards(): lax.psum_scatter(grad_outw, ('dp', 'seq'), scatter_dimension=0, tiled=True)  96.1 us
    all_gather x1, blocking collectives, shards(): lax.all_gather(vectors, ('dp', 'seq'), axis=0, tiled=True)  71.2 us
    all_to_all x1, waiting for transfers between devices, shards(): lax.all_to_all(key_vecs, 'seq', split_axis=1, concat_axis=0, tiled=True)  59.5 us
    all_to_all x1, blocking collectives, shards(): lax.all_to_all(grad_k.reshape(token_shape), 'seq', split_axis=0, concat_a...  54.6 us
  transfers between devices with their start and end apart: 15, of which 9 were waited for; matrix products, arithmetic and copies ran while one was open for 14% of the time, Pallas kernels for 0%

commit v1 on v0

--- a/solution.py
+++ b/solution.py
@@ -1,8 +1,11 @@
+import functools
 import math
 
 import jax
 import jax.numpy as jnp
 from jax import lax
+from jax.experimental import pallas as pl
+from jax.experimental.pallas import tpu as pltpu
 from jax.sharding import PartitionSpec as P
 
 HEAD_DIM = 64
@@ -85,7 +88,369 @@
     )
 
 
+MESH = pl.DeviceIdType.MESH
+LANES = 128
+F32 = jnp.float32
+BF16 = jnp.bfloat16
+
+
+class Grid:
+    def __init__(self, mesh):
+        dp, self.nz = mesh.shape["dp"], mesh.shape["seq"]
+        self.nc = 2 if dp % 2 == 0 else 1
+        rest = dp // self.nc
+        self.nx = max(k for k in range(1, math.isqrt(rest) + 1) if rest % k == 0)
+        self.ny = rest // self.nx
+        self.count = dp * self.nz
+
+    def here(self):
+        dp = lax.axis_index("dp")
+        self.z = lax.axis_index("seq")
+        self.c = dp % self.nc
+        self.x = (dp // self.nc) % self.nx
+        self.y = dp // (self.nc * self.nx)
+
+    def device(self, y, x, c, z):
+        return ((y * self.nx + x) * self.nc + c, z)
+
+    def off(self, axis, step):
+        return (getattr(self, axis) + step) % getattr(self, "n" + axis)
+
+    def peer(self, axis, step):
+        at = {name: getattr(self, name) for name in "yxcz"}
+        at[axis] = self.off(axis, step)
+        return self.device(**at)
+
+    def peers(self):
+        return [self.peer(axis, step) for axis in "zxyc" for step in range(1, getattr(self, "n" + axis))]
+
+
+def greet(grid):
+    barrier = pltpu.get_barrier_semaphore()
+    peers = grid.peers()
+    for peer in peers:
+        pl.semaphore_signal(barrier, inc=1, device_id=peer, device_id_type=MESH)
+    pl.semaphore_wait(barrier, len(peers))
+
+
+class Sems:
+    def __init__(self, send, recv):
+        self.send, self.recv, self.used = send, recv, 0
+
+    def remote(self, src, dst, device):
+        k = self.used
+        self.used += 1
+        return pltpu.make_async_remote_copy(
+            src_ref=src,
+            dst_ref=dst,
+            send_sem=self.send.at[k],
+            recv_sem=self.recv.at[k],
+            device_id=device,
+            device_id_type=MESH,
+        )
+
+
+def block_rows(start, size):
+    return pl.ds(pl.multiple_of(start * size, size), size)
+
+
+class Gather:
+    def __init__(self, grid, sems, local_sem, shard, full, cols):
+        self.grid, self.sems, self.local_sem = grid, sems, local_sem
+        self.shard, self.full, self.cols = shard, full, cols
+        self.rows = shard.shape[0]
+        self.half = self.rows * grid.nz // 2
+        self.sent = []
+
+    def go(self, copies):
+        for copy in copies:
+            copy.start()
+        self.sent += copies
+        self.flying = copies
+
+    def landed(self):
+        for copy in self.flying:
+            copy.wait_recv()
+
+    def start(self):
+        g = self.grid
+        own = self.full.at[g.y, g.x, g.c, block_rows(g.z, self.rows), self.cols]
+        src = self.shard.at[:, self.cols]
+        self.own = pltpu.make_async_copy(src, own, self.local_sem)
+        self.own.start()
+        self.go([self.sems.remote(src, own, g.peer("z", k)) for k in range(1, g.nz)])
+
+    def second(self):
+        g = self.grid
+        self.landed()
+        self.own.wait()
+        a = self.full.at[g.y, g.x, g.c, pl.ds(0, self.half), self.cols]
+        b = self.full.at[g.y, g.x, g.c, pl.ds(self.half, self.half), self.cols]
+        self.go(
+            [self.sems.remote(a, a, g.peer("x", k)) for k in range(1, g.nx)]
+            + [self.sems.remote(b, b, g.peer("y", k)) for k in range(1, g.ny)]
+        )
+
+    def third(self):
+        g = self.grid
+        self.landed()
+        a = self.full.at[g.y, :, g.c, pl.ds(0, self.half), self.cols]
+        b = self.full.at[:, g.x, g.c, pl.ds(self.half, self.half), self.cols]
+        self.go(
+            [self.sems.remote(a, a, g.peer("y", k)) for k in range(1, g.ny)]
+            + [self.sems.remote(b, b, g.peer("x", k)) for k in range(1, g.nx)]
+        )
+
+    def fourth(self):
+        g = self.grid
+        self.landed()
+        a = self.full.at[:, :, g.c, :, self.cols]
+        self.go([self.sems.remote(a, a, g.peer("c", k)) for k in range(1, g.nc)])
+
+    def finish(self):
+        self.landed()
+
+    def drain(self):
+        for copy in self.sent:
+            copy.wait_send()
+
+
+def gather_sems(grid):
+    return grid.nz - 1 + 2 * (grid.nx - 1) + 2 * (grid.ny - 1) + grid.nc - 1
+
+
+def pipeline(jobs, stages):
+    for tick in range(len(jobs) + len(stages) - 1):
+        for s in reversed(range(len(stages))):
+            if 0 <= tick - s < len(jobs):
+                getattr(jobs[tick - s], stages[s])()
+
+
+def gather_kernel(grid, blocks, *refs):
+    n = len(blocks)
+    shards, fulls, (send, recv, local) = refs[:n], refs[n : 2 * n], refs[2 * n :]
+    grid.here()
+    greet(grid)
+    sems = Sems(send, recv)
+    jobs = []
+    for shard, full, width in zip(shards, fulls, blocks):
+        for at in range(0, shard.shape[1], width):
+            jobs.append(Gather(grid, sems, local.at[len(jobs)], shard, full, pl.ds(at, width)))
+    pipeline(jobs, ["start", "second", "third", "fourth", "finish"])
+    for job in jobs:
+        job.drain()
+
+
+def gather_all(grid, shards, widths):
+    count = sum(s.shape[1] // w for s, w in zip(shards, widths))
+    any_spec = pl.BlockSpec(memory_space=pl.ANY)
+    return pl.pallas_call(
+        functools.partial(gather_kernel, grid, widths),
+        out_shape=[
+            jax.ShapeDtypeStruct((grid.ny, grid.nx, grid.nc, grid.nz * s.shape[0], s.shape[1]), s.dtype)
+            for s in shards
+        ],
+        in_specs=[any_spec] * len(shards),
+        out_specs=[any_spec] * len(shards),
+        scratch_shapes=[
+            pltpu.SemaphoreType.DMA((count * gather_sems(grid),)),
+            pltpu.SemaphoreType.DMA((count * gather_sems(grid),)),
+            pltpu.SemaphoreType.DMA((count,)),
+        ],
+        compiler_params=pltpu.CompilerParams(collective_id=1, has_side_effects=True),
+        name="gather_weights",
+    )(*shards)
+
+
+def add_into(dst, srcs, rows, step=32):
+    @pl.loop(0, rows // step)
+    def _(i):
+        at = block_rows(i, step)
+        total = dst[at, :].astype(F32)
+        for src in srcs:
+            total += src[at, :].astype(F32)
+        dst[at, :] = total.astype(dst.dtype)
+
+
+class Reduce:
+    def __init__(self, grid, sems, bufs):
+        self.grid, self.sems = grid, sems
+        self.sum, self.in2a, self.in2b, self.in3a, self.in3b, self.in4 = bufs
+        self.half = self.sum.shape[2] // 2
+        self.rows = self.sum.shape[2] // grid.nz
+        self.sent = []
+
+    go, landed, drain = Gather.go, Gather.landed, Gather.drain
+
+    def start(self, other):
+        g = self.grid
+        self.go([self.sems.remote(other, self.sum, g.peer("c", 1))])
+
+    def second(self, own):
+        g = self.grid
+        self.landed()
+        for y in range(g.ny):
+            for x in range(g.nx):
+                add_into(self.sum.at[y, x], [own.at[y, x]], 2 * self.half)
+        lo, hi = pl.ds(0, self.half), pl.ds(self.half, self.half)
+        self.go(
+            [
+                self.sems.remote(self.sum.at[g.off("y", k), :, lo], self.in2a.at[k - 1], g.peer("y", k))
+                for k in range(1, g.ny)
+            ]
+            + [
+                self.sems.remote(self.sum.at[:, g.off("x", k), hi], self.in2b.at[k - 1], g.peer("x", k))
+                for k in range(1, g.nx)
+            ]
+        )
+
+    def third(self):
+        g = self.grid
+        self.landed()
+        lo, hi = pl.ds(0, self.half), pl.ds(self.half, self.half)
+        for x in range(g.nx):
+            add_into(self.sum.at[g.y, x, lo], [self.in2a.at[k, x] for k in range(g.ny - 1)], self.half)
+        for y in range(g.ny):
+            add_into(self.sum.at[y, g.x, hi], [self.in2b.at[k, y] for k in range(g.nx - 1)], self.half)
+        self.go(
+            [
+                self.sems.remote(self.sum.at[g.y, g.off("x", k), lo], self.in3a.at[k - 1], g.peer("x", k))
+                for k in range(1, g.nx)
+            ]
+            + [
+                self.sems.remote(self.sum.at[g.off("y", k), g.x, hi], self.in3b.at[k - 1], g.peer("y", k))
+                for k in range(1, g.ny)
+            ]
+        )
+
+    def fourth(self):
+        g = self.grid
+        self.landed()
+        lo, hi = pl.ds(0, self.half), pl.ds(self.half, self.half)
+        add_into(self.sum.at[g.y, g.x, lo], [self.in3a.at[k] for k in range(g.nx - 1)], self.half)
+        add_into(self.sum.at[g.y, g.x, hi], [self.in3b.at[k] for k in range(g.ny - 1)], self.half)
+        self.go(
+            [
+                self.sems.remote(
+                    self.sum.at[g.y, g.x, block_rows(g.off("z", k), self.rows)], self.in4.at[k - 1], g.peer("z", k)
+                )
+                for k in range(1, g.nz)
+            ]
+        )
+
+    def finish(self, out, cols):
+        g = self.grid
+        self.landed()
+        total = self.sum[g.y, g.x, block_rows(g.z, self.rows), :].astype(F32)
+        for k in range(g.nz - 1):
+            total += self.in4[k].astype(F32)
+        out[:, cols] = total
+
+
+def reduce_bufs(grid, rows, width, count):
+    group, half = rows * grid.nz, rows * grid.nz // 2
+    ny, nx = grid.ny, grid.nx
+    return [
+        pltpu.VMEM((count, *shape, width), BF16)
+        for shape in (
+            (ny, nx, group),
+            (ny - 1, nx, half),
+            (nx - 1, ny, half),
+            (nx - 1, half),
+            (ny - 1, half),
+            (grid.nz - 1, rows),
+        )
+    ]
+
+
+def reduce_sems(grid):
+    return grid.nz - 1 + 2 * (grid.nx - 1) + 2 * (grid.ny - 1) + grid.nc - 1
+
+
+class Feed:
+    def __init__(self, job, grid, part, cols, own, own_sem, out):
+        self.job, self.grid, self.part, self.cols, self.own, self.own_sem, self.out = job, grid, part, cols, own, own_sem, out
+
+    def start(self):
+        g = self.grid
+        self.copy = pltpu.make_async_copy(self.part.at[:, :, g.c, :, self.cols], self.own, self.own_sem)
+        self.copy.start()
+        self.job.start(self.part.at[:, :, g.off("c", 1), :, self.cols])
+
+    def second(self):
+        self.copy.wait()
+        self.job.second(self.own)
+
+    def third(self):
+        self.job.third()
+
+    def fourth(self):
+        self.job.fourth()
+
+    def finish(self):
+        self.job.finish(self.out, self.cols)
+
+
+def reduce_kernel(grid, widths, *refs):
+    n = len(widths)
+    parts, outs, scratch = refs[:n], refs[n : 2 * n], refs[2 * n :]
+    send, recv, local = scratch[:3]
+    bufs = scratch[3:]
+    grid.here()
+    greet(grid)
+    sems = Sems(send, recv)
+    jobs = []
+    for i, (part, out, width) in enumerate(zip(parts, outs, widths)):
+        own, *mine = bufs[7 * i : 7 * i + 7]
+        for k in range(part.shape[4] // width):
+            job = Reduce(grid, sems, [b.at[k] for b in mine])
+            jobs.append(Feed(job, grid, part, pl.ds(k * width, width), own.at[k % 2], local.at[len(jobs)], out))
+    pipeline(jobs, ["start", "second", "third", "fourth", "finish"])
+    for feed in jobs:
+        feed.job.drain()
+
+
+def reduce_all(grid, parts, widths):
+    counts = [p.shape[4] // w for p, w in zip(parts, widths)]
+    rows = [p.shape[3] // grid.nz for p in parts]
+    scratch = []
+    for r, w, k in zip(rows, widths, counts):
+        scratch.append(pltpu.VMEM((2, grid.ny, grid.nx, r * grid.nz, w), BF16))
+        scratch += reduce_bufs(grid, r, w, k)
+    total = sum(counts)
+    return pl.pallas_call(
+        functools.partial(reduce_kernel, grid, widths),
+        out_shape=[jax.ShapeDtypeStruct((r, p.shape[4]), F32) for r, p in zip(rows, parts)],
+        in_specs=[pl.BlockSpec(memory_space=pl.ANY)] * len(parts),
+        out_specs=[pl.BlockSpec(memory_space=pltpu.VMEM)] * len(parts),
+        scratch_shapes=[
+            pltpu.SemaphoreType.DMA((total * reduce_sems(grid),)),
+            pltpu.SemaphoreType.DMA((total * reduce_sems(grid),)),
+            pltpu.SemaphoreType.DMA((total,)),
+            *scratch,
+        ],
+        compiler_params=pltpu.CompilerParams(collective_id=2, has_side_effects=True, vmem_limit_bytes=60 << 20),
+        name="reduce_gradients",
+    )(*parts)
+
+
+def gathered_by_xla(grid, shards):
+    return [lax.all_gather(s, ("dp", "seq"), axis=0, tiled=True) for s in shards]
+
+
+def fits(grid, inputs, qkv_weight):
+    return (
+        inputs.shape[0] % SLOT == 0
+        and qkv_weight.shape[0] % 32 == 0
+        and grid.nc == 2
+        and grid.nx > 1
+        and grid.ny > 1
+        and grid.nz > 1
+    )
+
+
 def shards(
+    grid,
     inputs,
     timestep,
     context_len,
@@ -97,43 +462,40 @@
     vectors,
     bias_ff,
 ):
-    qkv_full, out_full, in_full, back_full, vec_full, bias_full = (
-        lax.all_gather(qkv_weight, ("dp", "seq"), axis=0, tiled=True),
-        lax.all_gather(out_weight, ("dp", "seq"), axis=0, tiled=True),
-        lax.all_gather(in_weight, ("dp", "seq"), axis=0, tiled=True),
-        lax.all_gather(back_weight, ("dp", "seq"), axis=0, tiled=True),
-        lax.all_gather(vectors, ("dp", "seq"), axis=0, tiled=True),
-        lax.all_gather(bias_ff, ("dp", "seq"), axis=0, tiled=True),
-    )
+    use_kernels = fits(grid, inputs, qkv_weight)
+    rows = vectors.shape[0]
+    width = inputs.shape[1]
+    if use_kernels:
+        small = jnp.concatenate([vectors.T.reshape(-1), bias_ff])
+        small = jnp.pad(small, (0, 16 * LANES - small.size)).reshape(16, LANES)
+        full = gather_all(
+            grid, (small, qkv_weight, out_weight, in_weight, back_weight), (LANES, width, width, width, width // 4)
+        )
+        small_full, qkv_full, out_full, in_full, back_full = [f.reshape(-1, f.shape[-1]) for f in full]
+        small_full = small_full.reshape(grid.count, 16 * LANES)
+        vec_full = small_full[:, : 8 * rows].reshape(grid.count, 8, rows).transpose(0, 2, 1).reshape(width, 8)
+        bias_full = small_full[:, 8 * rows : 8 * rows + bias_ff.size].reshape(-1)
+    else:
+        qkv_full, out_full, in_full, back_full, vec_full, bias_full = gathered_by_xla(
+            grid, (qkv_weight, out_weight, in_weight, back_weight, vectors, bias_ff)
+        )
     vec_all = vec_full.astype(jnp.float32)
     bias_all = bias_full.astype(jnp.float32)
-    width = inputs.shape[1]
     resid_in = inputs.astype(jnp.float32) + timestep.astype(jnp.float32)
     layer_in = resid_in.astype(jnp.bfloat16)
     qkv_proj = jnp.dot(layer_in, qkv_full, preferred_element_type=jnp.float32)
     queries = (qkv_proj[:, :width] + vec_all[:, 0]).astype(jnp.bfloat16)
     key_vecs = qkv_proj[:, width : 2 * width].astype(jnp.bfloat16)
     values = (qkv_proj[:, 2 * width :] + vec_all[:, 1]).astype(jnp.bfloat16)
-    q_heads, k_heads, v_heads = (
-        lax.all_to_all(queries, "seq", split_axis=1, concat_axis=0, tiled=True),
-        lax.all_to_all(key_vecs, "seq", split_axis=1, concat_axis=0, tiled=True),
-        lax.all_to_all(values, "seq", split_axis=1, concat_axis=0, tiled=True),
-    )
-    slot_count = context_len.shape[1]
-    head_width = q_heads.shape[1]
-    slot_shape = (slot_count, SLOT, head_width // HEAD_DIM, HEAD_DIM)
-    live_lens = context_len[0] + BLOCK
-    q_slots = q_heads.reshape(slot_shape)
-    k_slots = k_heads.reshape(slot_shape)
-    v_slots = v_heads.reshape(slot_shape)
+    slot_count = inputs.shape[0] // SLOT
+    slot_shape = (slot_count, SLOT, width // HEAD_DIM, HEAD_DIM)
+    first = lax.axis_index("seq") * slot_count
+    live_lens = lax.dynamic_slice(context_len[0], (first,), (slot_count,)) + BLOCK
+    q_slots = queries.reshape(slot_shape)
+    k_slots = key_vecs.reshape(slot_shape)
+    v_slots = values.reshape(slot_shape)
     ctx_slots, log_totals = lax.map(slot_forward, (q_slots, k_slots, v_slots, live_lens))
-    ctx_tokens = lax.all_to_all(
-        ctx_slots.reshape(slot_count * SLOT, head_width),
-        "seq",
-        split_axis=0,
-        concat_axis=1,
-        tiled=True,
-    )
+    ctx_tokens = ctx_slots.reshape(slot_count * SLOT, width)
     attn_out = jnp.dot(ctx_tokens, out_full, preferred_element_type=jnp.float32) + vec_all[:, 2]
     normed_mid, unit_mid, inv_mid = norm_forward(resid_in + attn_out, vec_all[:, 4], vec_all[:, 5])
     mid_low = normed_mid.astype(jnp.bfloat16)
@@ -162,26 +524,20 @@
     grad_ctx = jnp.einsum(
         "te,de->td", attn_low, out_full, preferred_element_type=jnp.float32
     ).astype(jnp.bfloat16)
-    grad_ctx_heads = lax.all_to_all(grad_ctx, "seq", split_axis=1, concat_axis=0, tiled=True)
     grad_q, grad_k, grad_v = lax.map(
         slot_backward,
-        (q_slots, k_slots, v_slots, live_lens, log_totals, grad_ctx_heads.reshape(slot_shape)),
-    )
-    token_shape = (slot_count * SLOT, head_width)
-    grad_q_tok, grad_k_tok, grad_v_tok = (
-        lax.all_to_all(grad_q.reshape(token_shape), "seq", split_axis=0, concat_axis=1, tiled=True),
-        lax.all_to_all(grad_k.reshape(token_shape), "seq", split_axis=0, concat_axis=1, tiled=True),
-        lax.all_to_all(grad_v.reshape(token_shape), "seq", split_axis=0, concat_axis=1, tiled=True),
-    )
-    grad_proj = jnp.concatenate([grad_q_tok, grad_k_tok, grad_v_tok], axis=1)
+        (q_slots, k_slots, v_slots, live_lens, log_totals, grad_ctx.reshape(slot_shape)),
+    )
+    grad_proj = jnp.concatenate([g.reshape(slot_count * SLOT, width) for g in (grad_q, grad_k, grad_v)], axis=1)
     grad_qkvw = jnp.einsum("td,te->de", layer_in, grad_proj, preferred_element_type=jnp.float32)
     grad_input = grad_one + jnp.einsum(
         "te,de->td", grad_proj, qkv_full, preferred_element_type=jnp.float32
     )
-    vec_grads = jnp.stack(
+    bias_rows = jnp.sum(grad_proj.astype(jnp.float32), axis=0)
+    vec_rows = jnp.stack(
         [
-            jnp.sum(grad_q_tok.astype(jnp.float32), axis=0),
-            jnp.sum(grad_v_tok.astype(jnp.float32), axis=0),
+            bias_rows[:width],
+            bias_rows[2 * width :],
             jnp.sum(grad_one, axis=0),
             jnp.sum(grad_two, axis=0),
             gain_mid_grad,
@@ -189,22 +545,31 @@
             gain_out_grad,
             shift_out_grad,
         ],
-        axis=1,
-    )
-    share_qkv, share_out, share_in, share_back, share_vec, share_bias = (
-        lax.psum_scatter(grad_qkvw, ("dp", "seq"), scatter_dimension=0, tiled=True),
-        lax.psum_scatter(grad_outw, ("dp", "seq"), scatter_dimension=0, tiled=True),
-        lax.psum_scatter(grad_inw, ("dp", "seq"), scatter_dimension=0, tiled=True),
-        lax.psum_scatter(grad_backw, ("dp", "seq"), scatter_dimension=0, tiled=True),
-        lax.psum_scatter(vec_grads, ("dp", "seq"), scatter_dimension=0, tiled=True),
-        lax.psum_scatter(bias_grad, ("dp", "seq"), scatter_dimension=0, tiled=True),
-    )
+    )
+    if use_kernels:
+        by_owner = vec_rows.reshape(8, grid.count, rows).transpose(1, 0, 2).reshape(grid.count, 8 * rows)
+        small = jnp.concatenate([by_owner, bias_grad.reshape(grid.count, -1)], axis=1)
+        small = jnp.pad(small, ((0, 0), (0, 16 * LANES - small.shape[1]))).astype(jnp.bfloat16)
+        parts = [g.astype(jnp.bfloat16) for g in (grad_backw, grad_inw, grad_outw, grad_qkvw)]
+        parts.append(small.reshape(-1, LANES))
+        parts = [p.reshape(grid.ny, grid.nx, grid.nc, -1, p.shape[1]) for p in parts]
+        share_back, share_in, share_out, share_qkv, share_small = reduce_all(
+            grid, parts, (width // 4, width, width, width, LANES)
+        )
+        share_small = share_small.reshape(-1)
+        share_vec = share_small[: 8 * rows].reshape(8, rows).T
+        share_bias = share_small[8 * rows : 8 * rows + bias_ff.size]
+    else:
+        share_qkv, share_out, share_in, share_back, share_vec, share_bias = [
+            lax.psum_scatter(g, ("dp", "seq"), scatter_dimension=0, tiled=True)
+            for g in (grad_qkvw, grad_outw, grad_inw, grad_backw, vec_rows.T, bias_grad)
+        ]
     return (result, grad_input, share_qkv, share_out, share_in, share_back, share_vec, share_bias)
 
 
 def solution(mesh):
     return jax.shard_map(
-        shards,
+        functools.partial(shards, Grid(mesh)),
         mesh=mesh,
         in_specs=(
             P(("dp", "seq"), None),

time: 2090 us -> 734 us (0.35)
  waiting for transfers between devices: 1220 us -> 0 us
  blocking collectives: 319 us -> 0 us
  Pallas kernels: 0 us -> 289 us
  matrix products: 311 us -> 265 us
  local copies, waits for them, and re-layouts: 138 us -> 108 us
  starting transfers between devices: 26.9 us -> 0 us
    reduce_scatter x4 -> x0, waiting for transfers between devices: 989 us -> none  [the longest x1 366 us: shards(): lax.psum_scatter(grad_backw, ('dp', 'seq'), scatter_dimension=0, tiled=True)]
    pallas_call x0 -> x2, Pallas kernels: none -> 289 us  [the longest x1 148 us: gather_all(): pl.pallas_call(functools.partial(gather_kernel, grid, widths), out_shape=...]
    all_to_all x6 -> x0, waiting for transfers between devices: 232 us -> none  [the longest x1 59.5 us: shards(): lax.all_to_all(key_vecs, 'seq', split_axis=1, concat_axis=0, tiled=True)]
    all_gather x2 -> x0, blocking collectives: 176 us -> none  [the longest x1 105 us: shards(): lax.all_gather(bias_ff, ('dp', 'seq'), axis=0, tiled=True)]
    all_to_all x2 -> x0, blocking collectives: 101 us -> none  [the longest x1 54.6 us: shards(): lax.all_to_all(grad_k.reshape(token_shape), 'seq', split_axis=0, concat_a...]
    all_to_all x15 -> x0, local copies, waits for them, and re-layouts: 48.8 us -> none  [the longest x2 8.47 us: shards(): lax.all_to_all(key_vecs, 'seq', split_axis=1, concat_axis=0, tiled=True)]
    unnamed x1 -> x0, blocking collectives: 42 us -> none
    all_to_all x6 -> x0, starting transfers between devices: 26.6 us -> none  [the longest x1 4.85 us: shards(): lax.all_to_all(grad_q.reshape(token_shape), 'seq', split_axis=0, concat_a...]
  transfers between devices with their start and end apart: 15 -> 0, of which waited for: 9 -> 0; matrix products, arithmetic and copies ran while one was open for 14% -> 0% of each run, Pallas kernels for 0% -> 0%
where the time goes in v1:
time: 734 us; the launch traced here: 724 us
  Pallas kernels  289 us (39%)
  matrix products  265 us (36%)
  local copies, waits for them, and re-layouts  108 us (15%)
  other arithmetic  58.4 us (8%)
    pallas_call x1, Pallas kernels, gather_all(): pl.pallas_call(functools.partial(gather_kernel, grid, widths), out_shape=...  148 us
    pallas_call x1, Pallas kernels, reduce_all(): pl.pallas_call(functools.partial(reduce_kernel, grid, widths), out_shape=...  140 us
    dot_general x1, matrix products, shards(): jnp.dot(mid_low, in_full, preferred_element_type=jnp.float32) + bias_all  46 us
    dot_general x4, matrix products, slot_scores(): jnp.einsum('qhd,khd->hqk', queries, key_vecs, preferred_element_type=jnp....  35.9 us
    unnamed x111, local copies, waits for them, and re-layouts  29.5 us
    convert_element_type x2, other arithmetic, slot_backward(): grad_scores = (attn_exact * (grad_probs - row_dot)).astype(jnp.bfloat16)  23.3 us
    dot_general x1, matrix products, shards(): jnp.einsum('td,fd->tf', branch_low, back_full, preferred_element_type=jnp...  22.5 us
    while x4, local copies, waits for them, and re-layouts, shards(): lax.map(slot_forward, (q_slots, k_slots, v_slots, live_lens))  20.1 us

profile of v1, /device:TPU:0, one launch (start us, length us, event | category | flops | bytes accessed | tf_op | source)
XLA Modules:
  0.0 723.5 jit_solution(7767213642145611219)
XLA Ops:
  13.4 148.3 %gather_weights.1 = (bf16[2,2,2,64,128]{4,3,2,1,0:T(8,128)(2,1)}, bf16[2,2,2,128,3072]{4,3,2,1,0:T(8,128)(2,1)}, bf16[2,2,2,128,1024]{4,3,2,1,0:T(8,128)(2,1)}, ...) custom-call(bf16[16,128]{1,0:T(8,128)(2,1)} %fusion.98.refs_0_, bf16[32,3072]{1,0:T(8,128)(2,1)} %refs_1_.1, ...), custom_call_target="tpu_custom_call" | custom-call | tf_op jit(solution)/shard_map/gather_weights/pallas_call | solution.py:247
  164.2 9.7 %fusion.89 = f32[1024,3072]{1,0:T(8,128)S(1)} fusion(bf16[1024,3072]{1,0:T(8,128)(2,1)} %bitcast.229, bf16[1024,1024]{0,1:T(8,128)(2,1)} %copy.66, f32[1024]{0:T(1024)S(1)} %bitcast.219), kind=kOutput, calls=%fused_computation.126 | convolution fusion | flops 6445596672 | bytes 20975616 | tf_op jit(solution)/shard_map/dot_general | solution.py:486
  177.6 6.3 reshape.248
  183.9 5.4 copy.72
  193.3 4.5 copy.73
  197.7 6.4 reshape.247
  204.1 5.7 copy.71
  211.3 31.8 %while.26 = (s32[]{:T(128)}, bf16[2,512,16,64]{1,3,2,0:T(8,128)(2,1)}, f32[2,16,512]{2,1,0:T(8,128)S(1)}, bf16[2,512,16,64]{1,3,2,0:T(8,128)(2,1)}, s32[2]{0:T(1...) while((s32[]{:T(128)}, ...), condition=%wide.region_3.4_spmd, body=%wide.region_0.3_spmd.sunk | while | flops 1124590080 | bytes 79958216 | solution.py:497
  212.5 5.1 fusion.148
  228.1 5.1 fusion.148
  243.2 4.5 copy.74
  252.8 46.0 %fusion.54 = (bf16[1024,4096]{1,0:T(8,128)(2,1)}, f32[1024,4096]{1,0:T(8,128)}) fusion(f32[4096]{0:T(1024)S(1)} %copy-done.37, bf16[1024,4096]{1,0:T(8,128)(2,1)S(1)} %bitcast.226, bf16[1024,1024]{0,1:T(8,128)(2,1)S(1)} %fusion.101.clone.4), kind=kOutput, calls=%fused_computation.62 | convolution fusion | flops 8866758656 | bytes 35667968 | tf_op jit(solution)/shard_map/dot_general | solution.py:502
  298.8 15.8 %fusion.109 = (f32[1024]{0:T(1024)S(1)}, f32[1024,1024]{0,1:T(8,128)}) fusion(f32[1024]{0:T(1024)S(1)} %bitcast.216, bf16[1024,4096]{1,0:T(8,128)(2,1)} %get-tuple-element.263, bf16[4096,1024]{1,0:T(8,128)(2,1)} %bitcast.227, f32[1024]{0:T(1024)S(1)} %bitcast.210, f32[1024]{0:T(1024)S(1)} %bitcast.200, f32[1024]{0:T(1024)S(1)} %add_rsqrt_fusion.1, ...), kind=kOutput, calls=%fused_computation.167 | convolution fusion | flops 8597273600 | bytes 25190400 | tf_op jit(solution)/shard_map/dot_general | solution.py:504
  320.8 22.5 %fusion.110 = (bf16[4096]{0:T(1024)(128)(2,1)}, bf16[1024,4096]{1,0:T(8,128)(2,1)}) fusion(f32[1024,4096]{1,0:T(8,128)} %get-tuple-element.264, f32[4096]{0:T(1024)S(1)} %copy-done.37, bf16[4096,1024]{1,0:T(8,128)(2,1)} %bitcast.228, f32[1024]{0:T(1024)S(1)} %get-tuple-element.270, f32[1024,1024]{0,1:T(8,128)S(1)} %copy-done.4, ...), kind=kOutput, calls=%fused_computation.168 | convolution fusion | flops 8649699328 | bytes 39890944 | tf_op jit(solution)/shard_map/td,fd->tf/dot_general | solution.py:511
  343.2 16.7 %multiply_reduce_fusion.1 = (bf16[1024]{0:T(1024)(128)(2,1)S(1)}, f32[1024]{0:T(1024)S(1)}, f32[1024]{0:T(1024)S(1)}, bf16[1024]{0:T(1024)(128)(2,1)S(1)}, f32[1024,1024]{0,1:T(8,128)S(1)}) fusion(f32[1024,1024]{0,1:T(8,128)S(1)} %get-tuple-element.262, f32[1024]{0:T(1024)S(1)} %add_rsqrt_fusion.1, f32[1024]{0:T(1024)S(1)} %broadcast_multiply_fusion.5, ...), kind=kOutput, calls=%fused_computation.100 | convolution fusion | flops 8608804864 | bytes 31502336 | tf_op jit(solution)/shard_map/tf,df->td/dot_general | solution.py:516
  360.0 15.8 %convolution_convert_fusion.1 = bf16[4096,1024]{1,0:T(8,128)(2,1)} fusion(bf16[1024,4096]{1,0:T(8,128)(2,1)} %get-tuple-element.263, bf16[1024,1024]{0,1:T(8,128)(2,1)S(1)} %copy-done.6, f32[1024,1024]{0,1:T(8,128)S(1)} %copy-done.4, f32[1024]{0:T(1024)S(1)} %get-tuple-element.270, f32[1024]{0:T(1024)S(1)} %get-tuple-element.271, f32[1024]{0:T(1024)S(1)} %bitcast.207, ...), kind=kOutput, calls=%fused_computation.84 | convolution fusion | flops 8603566080 | bytes 23089152 | tf_op jit(solution)/shard_map/tf,td->fd/dot_general | solution.py:510
  381.5 16.4 %convolution_convert_fusion = bf16[1024,4096]{1,0:T(8,128)(2,1)} fusion(bf16[1024,4096]{1,0:T(8,128)(2,1)} %get-tuple-element.269, f32[1024,1024]{0,1:T(8,128)S(1)} %get-tuple-element.262, f32[1024]{0:T(1024)S(1)} %bitcast.211, f32[1024]{0:T(1024)S(1)} %bitcast.203, f32[1024]{0:T(1024)S(1)} %add_rsqrt_fusion.1, f32[1024]{0:T(1024)S(1)} %broadcast_multiply_fusion.5), kind=kOutput, calls=%fused_computation.83 | convolution fusion | flops 8599371776 | bytes 20987904 | tf_op jit(solution)/shard_map/td,tf->df/dot_general | solution.py:515
  411.4 5.4 copy.81
  421.6 103.7 %while.27 = (s32[]{:T(128)}, bf16[2,512,16,64]{1,3,2,0:T(8,128)(2,1)}, bf16[2,512,16,64]{1,3,2,0:T(8,128)(2,1)}, bf16[2,512,16,64]{1,3,2,0:T(8,128)(2,1)}, bf16[...) while((s32[]{:T(128)}, ...), condition=%wide.region_14.15_spmd, body=%wide.region_12.14_spmd.sunk | while | flops 2724717056 | bytes 170039568 | solution.py:527
  423.0 9.9 %fusion.159 = f32[16,512,512]{1,2,0:T(8,128)} fusion(bf16[2,512,16,64]{1,3,2,0:T(8,128)(2,1)} %get-tuple-element.441, s32[]{:T(128)S(6)} %copy.127, bf16[2,512,16,64]{1,3,2,0:T(8,128)(2,1)} %get-tuple-element.440), kind=kOutput, calls=%fused_computation.36.clone.1 | convolution fusion | flops 536870912 | bytes 18875392 | tf_op jit(solution)/shard_map/while/body/eval_jaxpr/qhd,khd->hqk/dot_general | solution.py:70
  433.0 12.9 %multiply_reduce_fusion.7 = (f32[16,512]{1,0:T(8,128)S(1)}, f32[16,512,512]{1,2,0:T(8,128)}) fusion(f32[16,512,512]{1,2,0:T(8,128)} %fusion.159, f32[16,512]{1,0:T(8,128)S(1)} %dynamic-slice_bitcast_fusion.2, bf16[2,512,16,64]{1,3,2,0:T(8,128)(2,1)S(1)} %get-tuple-element.436, s32[]{:T(128)S(6)} %copy.127, ...), kind=kOutput, calls=%fused_computation.23.clone.1 | convolution fusion | flops 557834240 | bytes 35718656 | tf_op jit(solution)/shard_map/while/body/eval_jaxpr/qhd,khd->hqk/dot_general | solution.py:47
  445.9 11.7 %multiply_convert_fusion.4 = bf16[16,512,512]{1,2,0:T(8,128)(2,1)S(1)} fusion(f32[16,512,512]{1,2,0:T(8,128)} %get-tuple-element.384, f32[16,512,512]{1,2,0:T(8,128)} %fusion.159, f32[16,512]{1,0:T(8,128)S(1)} %get-tuple-element.385), kind=kLoop, calls=%fused_computation.22.clone.1 | loop fusion | flops 12582912 | bytes 41975808 | tf_op jit(solution)/shard_map/while/body/eval_jaxpr/convert_element_type | solution.py:72
  457.6 9.5 %fusion.162 = bf16[2,512,16,64]{1,3,2,0:T(8,128)(2,1)} fusion(bf16[2,512,16,64]{1,3,2,0:T(8,128)(2,1)} %get-tuple-element.424, s32[]{:T(128)S(6)} %copy.127, f32[16,512,512]{1,2,0:T(8,128)} %get-tuple-element.384, bf16[2,512,16,64]{1,3,2,0:T(8,128)(2,1)S(1)} %copy-done.3), kind=kOutput, calls=%fused_computation.35.clone.1 | convolution fusion | flops 541589504 | bytes 18875392 | tf_op jit(solution)/shard_map/while/body/eval_jaxpr/hqk,qhd->khd/dot_general | solution.py:81
  474.7 9.9 %fusion.159 = f32[16,512,512]{1,2,0:T(8,128)} fusion(bf16[2,512,16,64]{1,3,2,0:T(8,128)(2,1)} %get-tuple-element.441, s32[]{:T(128)S(6)} %copy.127, bf16[2,512,16,64]{1,3,2,0:T(8,128)(2,1)} %get-tuple-element.440), kind=kOutput, calls=%fused_computation.36.clone.1 | convolution fusion | flops 536870912 | bytes 18875392 | tf_op jit(solution)/shard_map/while/body/eval_jaxpr/qhd,khd->hqk/dot_general | solution.py:70
  484.6 12.9 %multiply_reduce_fusion.7 = (f32[16,512]{1,0:T(8,128)S(1)}, f32[16,512,512]{1,2,0:T(8,128)}) fusion(f32[16,512,512]{1,2,0:T(8,128)} %fusion.159, f32[16,512]{1,0:T(8,128)S(1)} %dynamic-slice_bitcast_fusion.2, bf16[2,512,16,64]{1,3,2,0:T(8,128)(2,1)S(1)} %get-tuple-element.436, s32[]{:T(128)S(6)} %copy.127, ...), kind=kOutput, calls=%fused_computation.23.clone.1 | convolution fusion | flops 557834240 | bytes 35718656 | tf_op jit(solution)/shard_map/while/body/eval_jaxpr/qhd,khd->hqk/dot_general | solution.py:47
  497.5 11.7 %multiply_convert_fusion.4 = bf16[16,512,512]{1,2,0:T(8,128)(2,1)S(1)} fusion(f32[16,512,512]{1,2,0:T(8,128)} %get-tuple-element.384, f32[16,512,512]{1,2,0:T(8,128)} %fusion.159, f32[16,512]{1,0:T(8,128)S(1)} %get-tuple-element.385), kind=kLoop, calls=%fused_computation.22.clone.1 | loop fusion | flops 12582912 | bytes 41975808 | tf_op jit(solution)/shard_map/while/body/eval_jaxpr/convert_element_type | solution.py:72
  509.2 9.5 %fusion.162 = bf16[2,512,16,64]{1,3,2,0:T(8,128)(2,1)} fusion(bf16[2,512,16,64]{1,3,2,0:T(8,128)(2,1)} %get-tuple-element.424, s32[]{:T(128)S(6)} %copy.127, f32[16,512,512]{1,2,0:T(8,128)} %get-tuple-element.384, bf16[2,512,16,64]{1,3,2,0:T(8,128)(2,1)S(1)} %copy-done.3), kind=kOutput, calls=%fused_computation.35.clone.1 | convolution fusion | flops 541589504 | bytes 18875392 | tf_op jit(solution)/shard_map/while/body/eval_jaxpr/hqk,qhd->khd/dot_general | solution.py:81
  541.3 8.2 %convolution_add_fusion = f32[1024,1024]{0,1:T(8,128)} fusion(f32[1024,1024]{0,1:T(8,128)S(1)} %copy-done.15, bf16[1024,3072]{1,0:T(8,128)(2,1)S(1)} %bitcast.232, bf16[1024,3072]{0,1:T(8,128)(2,1)S(1)} %constant_dynamic-update-slice_fusion), kind=kOutput, calls=%fused_computation.119 | convolution fusion | flops 6443499520 | bytes 20971520 | tf_op jit(solution)/shard_map/te,de->td/dot_general | solution.py:533
  549.5 5.6 copy.89
  559.0 11.6 %convolution_convert_fusion.2 = bf16[1024,3072]{1,0:T(8,128)(2,1)} fusion(bf16[1024,3072]{0,1:T(8,128)(2,1)} %copy-done.7, bf16[1024,1024]{0,1:T(8,128)(2,1)S(1)} %copy-done.18, f32[1024]{0:T(1024)S(1)} %bitcast.221), kind=kOutput, calls=%fused_computation.85 | convolution fusion | flops 6448742400 | bytes 14684160 | tf_op jit(solution)/shard_map/td,te->de/dot_general | solution.py:532
  571.8 140.3 %reduce_gradients.1 = (f32[128,1024]{1,0:T(8,128)}, f32[32,4096]{1,0:T(8,128)}, f32[32,1024]{1,0:T(8,128)}, f32[32,3072]{1,0:T(8,128)}, f32[16,128]{1,0:T(8,128)}) custom-call(bf16[2,2,2,512,1024]{4,3,2,1,0:T(8,128)(2,1)} %bitcast.184, bf16[2,2,2,128,4096]{4,3,2,1,0:T(8,128)(2,1)} %bitcast.185, bf16[2,2,2,128,1024]{4,3,2,1,0:T(8,128)(2,1)} %bitcast.194, ...), custom_call_target="tpu_custom_call" | custom-call | tf_op jit(solution)/shard_map/reduce_gradients/pallas_call | solution.py:421
  714.6 5.5 copy.88
  (218 shorter events, 122.0 us)
Async XLA Ops:
  0.6 10.2 %copy-start.16 = (bf16[1024,1024]{1,0:T(8,128)(2,1)S(1)}, bf16[1024,1024]{1,0:T(8,128)(2,1)}, u32[]{:S(2)}) copy-start(bf16[1024,1024]{1,0:T(8,128)(2,1)} %param.14) | copy-start | bytes 6291460
  6.2 158.0 %copy-start.41 = (f32[1,1024]{1,0:T(1,128)}, f32[1,1024]{1,0:T(1,128)S(1)}, u32[]{:S(2)}) copy-start(f32[1,1024]{1,0:T(1,128)S(1)} %add.184) | copy-start | bytes 12292
  243.1 5.2 copy-start
  243.1 5.2 copy-start.23
  243.1 5.2 copy-start.46
  243.2 5.2 copy-start.17
  243.2 5.2 copy-start.40
  243.2 5.2 copy-start.42
  243.2 5.2 copy-start.44
  247.7 5.0 slice-start
  252.8 46.0 %copy-start.39 = (f32[1024,1]{0,1:T(1,128)S(1)}, f32[1024,1]{0,1:T(1,128)}, u32[]{:S(2)}) copy-start(f32[1024,1]{0,1:T(1,128)} %get-tuple-element.253) | copy-start | bytes 12292
  343.2 16.7 %copy-start.6 = (bf16[1024,1024]{0,1:T(8,128)(2,1)S(1)}, bf16[1024,1024]{0,1:T(8,128)(2,1)}, u32[]{:S(2)}) copy-start(bf16[1024,1024]{0,1:T(8,128)(2,1)} %copy.76) | copy-start | bytes 6291460
  360.0 15.8 %copy-start.36 = (f32[1024,1]{0,1:T(1,128)S(1)}, f32[1024,1]{0,1:T(1,128)}, u32[]{:S(2)}) copy-start(f32[1024,1]{0,1:T(1,128)} %get-tuple-element.252) | copy-start | bytes 12292
  381.5 20.2 %copy-start.14 = (f32[1024,1024]{0,1:T(8,128)}, f32[1024,1024]{0,1:T(8,128)S(1)}, u32[]{:S(2)}) copy-start(f32[1024,1024]{0,1:T(8,128)S(1)} %get-tuple-element.243) | copy-start | bytes 12582916
  381.5 16.5 %copy-start.20 = (bf16[128,8,2,512]{3,1,2,0:T(8,128)(2,1)S(1)}, bf16[128,8,2,512]{3,1,2,0:T(8,128)(2,1)}, u32[]{:S(2)}) copy-start(bf16[128,8,2,512]{3,1,2,0:T(8,128)(2,1)} %copy-done.19) | copy-start | bytes 6291460
  416.8 4.8 copy-start.47
  423.0 9.9 %copy-start.2 = (bf16[2,512,16,64]{1,3,2,0:T(8,128)(2,1)S(1)}, bf16[2,512,16,64]{1,3,2,0:T(8,128)(2,1)}, u32[]{:S(2)}) copy-start(bf16[2,512,16,64]{1,3,2,0:T(8,128)(2,1)} %get-tuple-element.438) | copy-start | bytes 6291460 | tf_op jit(solution)/shard_map/while
  445.9 11.7 %copy-start.3 = (bf16[2,512,16,64]{1,3,2,0:T(8,128)(2,1)S(1)}, bf16[2,512,16,64]{1,3,2,0:T(8,128)(2,1)}, u32[]{:S(2)}) copy-start(bf16[2,512,16,64]{1,3,2,0:T(8,128)(2,1)} %get-tuple-element.440) | copy-start | bytes 6291460 | tf_op jit(solution)/shard_map/while
  474.7 9.9 %copy-start.2 = (bf16[2,512,16,64]{1,3,2,0:T(8,128)(2,1)S(1)}, bf16[2,512,16,64]{1,3,2,0:T(8,128)(2,1)}, u32[]{:S(2)}) copy-start(bf16[2,512,16,64]{1,3,2,0:T(8,128)(2,1)} %get-tuple-element.438) | copy-start | bytes 6291460 | tf_op jit(solution)/shard_map/while
  497.5 11.7 %copy-start.3 = (bf16[2,512,16,64]{1,3,2,0:T(8,128)(2,1)S(1)}, bf16[2,512,16,64]{1,3,2,0:T(8,128)(2,1)}, u32[]{:S(2)}) copy-start(bf16[2,512,16,64]{1,3,2,0:T(8,128)(2,1)} %get-tuple-element.440) | copy-start | bytes 6291460 | tf_op jit(solution)/shard_map/while
  535.5 5.8 copy-start.15
  558.9 11.9 %copy-start.33 = (bf16[1,32,32]{2,1,0:T(8,128)(2,1)S(1)}, bf16[1,32,32]{2,1,0:T(8,128)(2,1)}, u32[]{:S(2)}) copy-start(bf16[1,32,32]{2,1,0:T(8,128)(2,1)} %stack.29) | copy-start | bytes 6148
  558.9 11.9 %copy-start.34 = (bf16[1,32,32]{2,1,0:T(8,128)(2,1)S(1)}, bf16[1,32,32]{2,1,0:T(8,128)(2,1)}, u32[]{:S(2)}) copy-start(bf16[1,32,32]{2,1,0:T(8,128)(2,1)} %stack.30) | copy-start | bytes 6148
  558.9 11.9 %copy-start.31 = (bf16[1,32,32]{2,1,0:T(8,128)(2,1)S(1)}, bf16[1,32,32]{2,1,0:T(8,128)(2,1)}, u32[]{:S(2)}) copy-start(bf16[1,32,32]{2,1,0:T(8,128)(2,1)} %stack.31) | copy-start | bytes 6148
  558.9 11.9 %copy-start.32 = (bf16[1,32,32]{2,1,0:T(8,128)(2,1)S(1)}, bf16[1,32,32]{2,1,0:T(8,128)(2,1)}, u32[]{:S(2)}) copy-start(bf16[1,32,32]{2,1,0:T(8,128)(2,1)} %stack.32) | copy-start | bytes 6148
  559.0 11.9 %copy-start.30 = (bf16[1,32,32]{2,1,0:T(8,128)(2,1)S(1)}, bf16[1,32,32]{2,1,0:T(8,128)(2,1)}, u32[]{:S(2)}) copy-start(bf16[1,32,32]{2,1,0:T(8,128)(2,1)} %stack.33) | copy-start | bytes 6148
  559.0 11.9 %copy-start.29 = (bf16[1,32,32]{2,1,0:T(8,128)(2,1)S(1)}, bf16[1,32,32]{2,1,0:T(8,128)(2,1)}, u32[]{:S(2)}) copy-start(bf16[1,32,32]{2,1,0:T(8,128)(2,1)} %stack.34) | copy-start | bytes 6148
  559.0 12.1 %copy-start.38 = (bf16[4096]{0:T(1024)(128)(2,1)S(1)}, bf16[4096]{0:T(1024)(128)(2,1)}, u32[]{:S(2)}) copy-start(bf16[4096]{0:T(1024)(128)(2,1)} %get-tuple-element.268) | copy-start | bytes 24580
  714.6 5.5 copy-start.25
  714.6 6.2 copy-start.26
  714.6 6.9 copy-start.22
  714.6 7.7 %copy-start.21 = (f32[128,1024]{1,0:T(8,128)S(1)}, f32[128,1024]{1,0:T(8,128)}, u32[]{:S(2)}) copy-start(f32[128,1024]{1,0:T(8,128)} %get-tuple-element.456) | copy-start | bytes 1572868
  (27 other events, 84.5 us)
